TPU v7x, 32 devices: a whole 2x2x4 slice. The times are simulated.
32 devices in a mesh: group: 2 (over y), seq: 8 (over z, x), chan: 2 (over core).
Axes of the slice: x: 2, y: 2, z: 4, core: 2. Of those that a mesh axis runs over, the one named last changes fastest.
Arguments:
- fresh: bfloat16 [2048, 3, 2048], P(('group', 'seq'), None, 'chan'), parts along dimension 0, may hold values from -6 to 6
- library: bfloat16 [8, 8, 2048], P('seq', None, 'chan'), may hold values from -6 to 6
- block_slot: int32 [8], replicated, may hold values from 0 to 7, each once
- prefix_blocks: int32 [16, 4], P('group'), parts along dimension 0, may hold values from 0 to 7, all different within a row
- short_taps: float32 [3, 3, 2048], P(None, None, 'chan'), may hold values from -4 to 4
- long_filter: float32 [1024, 2048], P('seq', 'chan'), may hold values from -2 to 2
- skip_gain: float32 [2048], P('chan'), may hold values from -6 to 6
Outputs:
- mixed: bfloat16 [2048, 2048], P(('group', 'seq'), 'chan'), parts along dimension 0
There are 2 independent parts, one for each index of `group`. A program takes and returns all parts, laid end to end along the dimension named above; an argument that names none is the same for every part. Nothing has to cross between parts.
Inputs may be any that keep to these rules, and one draw needn't show every extreme that they name: `block_slot`: each number appears once. `prefix_blocks`: every library block is named at least once; the four entries of a row differ.
All inputs are finite; a program needn't handle non-finite values.
Results may differ from a plain program's by a relative error of at most 0.008.
Values may be sent and summed in bfloat16 or wider, within the bound.
A program may use at most 64 MiB of HBM per device.

v0:
```python
import functools
import math

import jax
import jax.numpy as jnp
import numpy as np
from jax import lax
from jax.experimental import pallas as pl
from jax.experimental.pallas import tpu as pltpu
from jax.sharding import PartitionSpec as P

TAPS = 3
BLK = 8


def from_behind(shard, axis, by):
    count = lax.axis_size(axis)
    pairs = [(i, i + by) for i in range(count) if 0 <= i + by < count]
    return lax.ppermute(shard, axis, pairs)


def exact_dot(pattern, matrix, tensor):
    return jnp.einsum(pattern, matrix, tensor, precision=lax.Precision.HIGHEST)


def turn_angles(numbers, period):
    return (numbers % period).astype(jnp.float32) * (2.0 * math.pi / period)


def long_body(fresh, library, block_slot, prefix_blocks, short_taps, long_filter, skip_gain):
    row_count = fresh.shape[0]
    channels = fresh.shape[2]
    devices = lax.axis_size("seq")
    seq_index = lax.axis_index("seq")
    group_rows = row_count // devices
    period = 2 * row_count * devices
    block_ids = jnp.arange(devices, dtype=jnp.int32)
    mode_ids = jnp.arange(2 * devices, dtype=jnp.int32)
    coarse = turn_angles(mode_ids[:, None] * block_ids[None, :], 2 * devices)
    cos_q = jnp.cos(coarse)
    sin_q = jnp.sin(coarse)
    local_rows = seq_index * group_rows + jnp.arange(group_rows, dtype=jnp.int32)
    twist = turn_angles(mode_ids[:, None] * local_rows[None, :], period)
    twist_cos = jnp.cos(twist)[:, :, None]
    twist_sin = jnp.sin(twist)[:, :, None]
    row_ids = jnp.arange(row_count, dtype=jnp.int32)
    fine_angles = turn_angles(row_ids[:, None] * row_ids[None, :], row_count)
    cos_m = jnp.cos(fine_angles)
    sin_m = jnp.sin(fine_angles)
    first_modes = 2 * seq_index + jnp.arange(2, dtype=jnp.int32)
    back_twist = turn_angles(first_modes[:, None] * row_ids[None, :], period)
    back_cos = jnp.cos(back_twist)[:, :, None]
    back_sin = jnp.sin(back_twist)[:, :, None]

    def to_modes(column):
        real_part = exact_dot("kq,qgc->kgc", cos_q, column)
        imag_part = -exact_dot("kq,qgc->kgc", sin_q, column)
        return jnp.stack(
            [
                real_part * twist_cos + imag_part * twist_sin,
                imag_part * twist_cos - real_part * twist_sin,
            ]
        )

    def to_spectrum(spread):
        real_part = exact_dot("ki,jic->jkc", cos_m, spread[0]) + exact_dot(
            "ki,jic->jkc", sin_m, spread[1]
        )
        imag_part = exact_dot("ki,jic->jkc", cos_m, spread[1]) - exact_dot(
            "ki,jic->jkc", sin_m, spread[0]
        )
        return (real_part, imag_part)

    blocks_here = row_count // BLK
    flat_ids = prefix_blocks.reshape(-1)
    first_block = jnp.minimum(seq_index * blocks_here, flat_ids.shape[0] - blocks_here)
    own_ids = lax.dynamic_slice_in_dim(flat_ids, first_block, blocks_here)
    matches = own_ids[:, None] == jnp.arange(block_slot.shape[0], dtype=jnp.int32)[None, :]
    wanted = jnp.sum(jnp.where(matches, block_slot[None, :], 0), axis=1)
    shards = lax.all_gather(library, "seq", axis=0, tiled=True)
    picker = (wanted[:, None] == jnp.arange(shards.shape[0], dtype=jnp.int32)[None, :]).astype(
        jnp.bfloat16
    )
    gathered = jnp.einsum("bn,nlc->blc", picker, shards, preferred_element_type=jnp.float32)
    cached = gathered.reshape(row_count, channels).astype(jnp.bfloat16)
    values = jnp.where(seq_index < devices // 4, cached, fresh[:, 2])
    stacked = jnp.concatenate([fresh[:, :2], values[:, None]], axis=1)
    previous = from_behind(stacked[row_count - (TAPS - 1) :], "seq", 1)
    extended = jnp.concatenate([previous, stacked], axis=0)
    shortened = jnp.zeros((row_count, 3, channels), jnp.float32)
    for offset in range(TAPS):
        window_start = TAPS - 1 - offset
        shortened = shortened + short_taps[offset][None] * extended[
            window_start : window_start + row_count
        ].astype(jnp.float32)
    gating = shortened[:, 0]
    signal = shortened[:, 1] * shortened[:, 2]
    spread_signal = to_modes(
        lax.all_to_all(signal[None], "seq", split_axis=1, concat_axis=0, tiled=True)
    )
    spread_taps = to_modes(
        lax.all_to_all(long_filter[None], "seq", split_axis=1, concat_axis=0, tiled=True)
    )
    moved_signal, moved_taps = (
        lax.all_to_all(
            spread_signal.astype(jnp.bfloat16), "seq", split_axis=1, concat_axis=2, tiled=True
        ).astype(spread_signal.dtype),
        lax.all_to_all(
            spread_taps.astype(jnp.bfloat16), "seq", split_axis=1, concat_axis=2, tiled=True
        ).astype(spread_taps.dtype),
    )
    sig_real, sig_imag = to_spectrum(moved_signal)
    tap_real, tap_imag = to_spectrum(moved_taps)
    prod_real = sig_real * tap_real - sig_imag * tap_imag
    prod_imag = sig_real * tap_imag + sig_imag * tap_real
    back_real = exact_dot("ki,jic->jkc", cos_m, prod_real) - exact_dot(
        "ki,jic->jkc", sin_m, prod_imag
    )
    back_imag = exact_dot("ki,jic->jkc", cos_m, prod_imag) + exact_dot(
        "ki,jic->jkc", sin_m, prod_real
    )
    turned = jnp.stack(
        [back_real * back_cos - back_imag * back_sin, back_imag * back_cos + back_real * back_sin]
    )
    spread = lax.all_to_all(turned, "seq", split_axis=2, concat_axis=1, tiled=True)
    positions = (
        exact_dot("kq,kgc->qgc", cos_q, spread[0]) - exact_dot("kq,kgc->qgc", sin_q, spread[1])
    ) / period
    convolved = lax.all_to_all(positions, "seq", split_axis=0, concat_axis=1, tiled=True)[0]
    output = gating * (convolved + skip_gain[None, :] * signal)
    return output.astype(jnp.bfloat16)


LANES = 128
FILTER, SIGNAL, BACK, SHELF = 0, 1, 2, 3


def wave_tables(tokens):
    steps = (2 * np.arange(tokens)[:, None] + 1) * np.arange(tokens)[None, :] % (4 * tokens)
    angles = steps.astype(np.float64) * (math.pi / (2 * tokens))
    table = np.concatenate([np.cos(angles), np.sin(angles)], axis=0)
    bf16 = jnp.bfloat16
    high = table.astype(np.float32).astype(bf16)
    low = (table - high.astype(np.float64)).astype(np.float32).astype(bf16)
    return high, low, np.ascontiguousarray(high.T)


def fused_kernel(
    n, pdev, x_ref, lib_ref, slot_ref, pref_ref, taps_ref, filt_ref, skip_ref, fhi_hbm, flo_hbm, g_hbm,
    out_ref,
    fhi, flo, gmat, hsend, hrecv, ssend, srecv, ysend, yrecv, libsend, libg, lastsend, lastg,
    halosend, halorecv, ext, gate, cach, hspec, prod,
    load_sem, send_sem, recv_sem, halo_send, halo_recv, last_send, last_recv,
):
    f32, bf16 = jnp.float32, jnp.bfloat16
    rows = x_ref.shape[1]
    tokens = rows * n
    prefix = pdev * rows
    me = lax.axis_index("seq")
    loads = [
        pltpu.make_async_copy(src, dst, load_sem.at[i])
        for i, (src, dst) in enumerate([(fhi_hbm, fhi), (flo_hbm, flo), (g_hbm, gmat)])
    ]
    for load in loads:
        load.start()

    barrier = pltpu.get_barrier_semaphore()
    for d in range(1, n):
        pl.semaphore_signal(
            barrier, inc=1, device_id={"seq": lax.rem(me + d, n)}, device_id_type=pl.DeviceIdType.MESH
        )

    def remote(src, dst, send, recv, peer):
        return pltpu.make_async_remote_copy(
            src_ref=src, dst_ref=dst, send_sem=send, recv_sem=recv,
            device_id={"seq": peer}, device_id_type=pl.DeviceIdType.MESH,
        )

    def at_rows(ref, index):
        return ref.at[pl.ds(pl.multiple_of(index * rows, rows), rows)]

    def move(kind, d):
        peer = lax.rem(me + d, n)
        source, target = {
            FILTER: (hsend.at[peer], at_rows(hrecv, me)),
            SIGNAL: (ssend.at[peer], at_rows(srecv, me)),
            BACK: (ysend.at[peer], yrecv.at[me]),
            SHELF: (libsend.at[peer], libg.at[me]),
        }[kind]
        return remote(source, target, send_sem.at[kind, d], recv_sem.at[kind, d], peer)

    def arrived(kind):
        for d in range(1, n):
            move(kind, d).wait_recv()

    halo_copy = remote(halosend, halorecv, halo_send, halo_recv, lax.rem(me + 1, n))
    others = [s for s in range(n) if s != pdev]
    last_copy = {
        s: remote(lastsend, lastg.at[me], last_send, last_recv.at[s], pdev) for s in others
    }

    for j in range(3):
        halosend[2 * j : 2 * j + 2] = x_ref[j, rows - 16 :].astype(f32)[14:]
    halosend[6:] = jnp.zeros((2, halosend.shape[1]), f32)
    shelf = lib_ref[0].astype(f32)
    for j in range(n):
        cols = slice(j * LANES, (j + 1) * LANES)
        libsend[j] = shelf[:, cols]
        lastsend[2 * j : 2 * j + 2] = shelf[6:, cols]
        hsend[j] = filt_ref[:, cols].astype(bf16)
    libg[me] = libsend[me]
    lastg[me] = lastsend[...]

    pl.semaphore_wait(barrier, n - 1)

    @pl.when(me < n - 1)
    def _():
        halo_copy.start()

    for s in others:
        @pl.when(me == s)
        def _():
            last_copy[s].start()

    for d in range(1, n):
        move(SHELF, d).start()
    for d in range(1, n):
        move(FILTER, d).start()
    at_rows(hrecv, me)[...] = hsend[me]
    for j in range(3):
        ext[j, 8:] = x_ref[j].astype(f32)

    @pl.when(me == 0)
    def _():
        halorecv[...] = jnp.zeros_like(halorecv)

    @pl.when(me > 0)
    def _():
        halo_copy.wait_recv()

    for j in range(3):
        ext[j, 6:8] = halorecv[2 * j : 2 * j + 2]

    per_row = pref_ref.shape[1]

    def wanted(b):
        return slot_ref[pref_ref[b // per_row, b % per_row]]

    blocks = prefix // BLK

    @pl.when(me == pdev)
    def _():
        for s in others:
            last_copy[s].wait_recv()
        ends = lastg[wanted(blocks - 1)]
        for j in range(n):
            ext[2, 6:8, j * LANES : (j + 1) * LANES] = ends[2 * j : 2 * j + 2]

    def short(j, cols):
        return (
            taps_ref[0, j : j + 1, cols] * ext[j, 8:, cols]
            + taps_ref[1, j : j + 1, cols] * ext[j, 7 : 7 + rows, cols]
            + taps_ref[2, j : j + 1, cols] * ext[j, 6 : 6 + rows, cols]
        )

    in_prefix = me < pdev
    for j in range(n):
        cols = slice(j * LANES, (j + 1) * LANES)
        factor = jnp.where(in_prefix, jnp.float32(1.0), short(2, cols))
        ssend[j] = (short(1, cols) * factor).astype(bf16)
    for d in range(1, n):
        move(SIGNAL, d).start()
    at_rows(srecv, me)[...] = ssend[me]
    for j in range(n):
        cols = slice(j * LANES, (j + 1) * LANES)
        gate[:, cols] = short(0, cols)

    own = pl.ds(pl.multiple_of(me * LANES, LANES), LANES)
    arrived(SHELF)
    cach[:8] = jnp.zeros((8, LANES), f32)
    for b in range(blocks):
        cach[8 + BLK * b : 8 + BLK * (b + 1)] = libg[wanted(b)]

    arrived(FILTER)
    for load in loads:
        load.wait()
    tile = 512
    skip = skip_ref[:, own]

    def filter_tile(i, carry):
        span = pl.ds(pl.multiple_of(i * tile, tile), tile)
        spec = jnp.dot(fhi[span], hrecv[...], preferred_element_type=f32)
        spec += jnp.dot(flo[span], hrecv[...], preferred_element_type=f32)
        hspec[span] = spec + jnp.where(i < tokens // tile, skip, 0.0)
        return carry

    lax.fori_loop(0, 2 * tokens // tile, filter_tile, 0)

    arrived(SIGNAL)
    cached = (
        taps_ref[0, 2:3, own] * cach[8:]
        + taps_ref[1, 2:3, own] * cach[7 : 7 + prefix]
        + taps_ref[2, 2:3, own] * cach[6 : 6 + prefix]
    )
    srecv[:prefix] = (srecv[:prefix].astype(f32) * cached).astype(bf16)

    half = 256

    def signal_tile(i, carry):
        upper = pl.ds(pl.multiple_of(i * half, half), half)
        lower = pl.ds(pl.multiple_of(tokens + i * half, half), half)
        even = jnp.dot(fhi[upper], srecv[...], preferred_element_type=f32)
        even += jnp.dot(flo[upper], srecv[...], preferred_element_type=f32)
        odd = jnp.dot(fhi[lower], srecv[...], preferred_element_type=f32)
        odd += jnp.dot(flo[lower], srecv[...], preferred_element_type=f32)
        tap_even, tap_odd = hspec[upper] * (1.0 / tokens), hspec[lower] * (1.0 / tokens)
        for span, value in (
            (upper, even * tap_even - odd * tap_odd),
            (lower, even * tap_odd + odd * tap_even),
        ):
            high = value.astype(bf16)
            prod[span, :LANES] = high
            prod[span, LANES:] = (value - high.astype(f32)).astype(bf16)
        return carry

    lax.fori_loop(0, tokens // half, signal_tile, 0)

    pair = 2 * rows

    def back_tile(i, carry):
        span = pl.ds(pl.multiple_of(i * pair, pair), pair)
        both = jnp.dot(gmat[span], prod[...], preferred_element_type=f32)
        value = (both[:, :LANES] + both[:, LANES:]).astype(bf16)
        ysend[2 * i] = value[:rows]
        ysend[2 * i + 1] = value[rows:]
        return carry

    lax.fori_loop(0, n // 2, back_tile, 0)
    for d in range(1, n):
        move(BACK, d).start()
    yrecv[me] = ysend[me]
    arrived(BACK)
    for j in range(n):
        cols = slice(j * LANES, (j + 1) * LANES)
        out_ref[:, cols] = (gate[:, cols] * yrecv[j].astype(f32)).astype(bf16)

    @pl.when(me < n - 1)
    def _():
        halo_copy.wait_send()

    @pl.when(me != pdev)
    def _():
        last_copy[others[0]].wait_send()

    for kind in (SHELF, FILTER, SIGNAL, BACK):
        for d in range(1, n):
            move(kind, d).wait_send()


def fused_body(n, fresh, library, block_slot, prefix_blocks, short_taps, long_filter, skip_gain):
    rows, channels = fresh.shape[0], fresh.shape[2]
    tokens = rows * n
    prefix = prefix_blocks.size * BLK
    f32, bf16 = jnp.float32, jnp.bfloat16
    high, low, turned = wave_tables(tokens)
    vmem = pl.BlockSpec(memory_space=pltpu.VMEM)
    smem = pl.BlockSpec(memory_space=pltpu.SMEM)
    far = pl.BlockSpec(memory_space=pl.ANY)
    dma = pltpu.SemaphoreType.DMA
    return pl.pallas_call(
        functools.partial(fused_kernel, n, prefix // rows),
        out_shape=jax.ShapeDtypeStruct((rows, channels), bf16),
        in_specs=[vmem, vmem, smem, smem, vmem, vmem, vmem, far, far, far],
        out_specs=vmem,
        scratch_shapes=[
            pltpu.VMEM((2 * tokens, tokens), bf16),
            pltpu.VMEM((2 * tokens, tokens), bf16),
            pltpu.VMEM((tokens, 2 * tokens), bf16),
            pltpu.VMEM((n, rows, LANES), bf16),
            pltpu.VMEM((tokens, LANES), bf16),
            pltpu.VMEM((n, rows, LANES), bf16),
            pltpu.VMEM((tokens, LANES), bf16),
            pltpu.VMEM((n, rows, LANES), bf16),
            pltpu.VMEM((n, rows, LANES), bf16),
            pltpu.VMEM((n, BLK, LANES), f32),
            pltpu.VMEM((n, BLK, LANES), f32),
            pltpu.VMEM((2 * n, LANES), f32),
            pltpu.VMEM((n, 2 * n, LANES), f32),
            pltpu.VMEM((8, channels), f32),
            pltpu.VMEM((8, channels), f32),
            pltpu.VMEM((3, rows + 8, channels), f32),
            pltpu.VMEM((rows, channels), f32),
            pltpu.VMEM((prefix + 8, LANES), f32),
            pltpu.VMEM((2 * tokens, LANES), f32),
            pltpu.VMEM((2 * tokens, 2 * LANES), bf16),
            dma((3,)),
            dma((4, n)),
            dma((4, n)),
            dma(()),
            dma(()),
            dma(()),
            dma((n,)),
        ],
        compiler_params=pltpu.CompilerParams(
            collective_id=0, has_side_effects=True, vmem_limit_bytes=50 * 1024 * 1024
        ),
    )(
        jnp.transpose(fresh, (1, 0, 2)), library, block_slot, prefix_blocks, short_taps, long_filter,
        skip_gain[None, :], jnp.asarray(high), jnp.asarray(low), jnp.asarray(turned),
    )


def body(n, fresh, library, block_slot, prefix_blocks, short_taps, long_filter, skip_gain):
    rows, channels = fresh.shape[0], fresh.shape[2]
    prefix = prefix_blocks.size * BLK
    small = (
        rows * n <= 1024
        and rows % 128 == 0
        and channels == n * LANES
        and library.shape[0] == 1
        and prefix % rows == 0
        and 0 < prefix // rows < n
    )
    chosen = functools.partial(fused_body, n) if small else long_body
    return chosen(fresh, library, block_slot, prefix_blocks, short_taps, long_filter, skip_gain)


def solution(mesh):
    return jax.shard_map(
        functools.partial(body, mesh.shape["seq"]),
        mesh=mesh,
        in_specs=(
            P(("group", "seq"), None, "chan"),
            P("seq", None, "chan"),
            P(),
            P("group", None),
            P(None, None, "chan"),
            P("seq", "chan"),
            P("chan"),
        ),
        out_specs=P(("group", "seq"), "chan"),
        check_vma=False,
    )
```

profile of v0, /device:TPU:0, one launch (start us, length us, event | category | flops | bytes accessed | tf_op | source)
XLA Modules:
  0.0 37.8 jit_solution(6386767905493863971)
XLA Ops:
  0.0 0.8 %copy.11.pref_ref = s32[8,4]{1,0:T(8,128)S(1)} copy(s32[8,4]{0,1:T(4,128)} %param.13) | data formatting | bytes 256 | tf_op args[3]
  0.8 0.0 copy-start
  0.8 1.1 %copy-done = bf16[128,3,1024]{2,0,1:T(8,128)(2,1)S(1)} copy-done((bf16[128,3,1024]{2,0,1:T(8,128)(2,1)S(1)}, bf16[128,3,1024]{2,0,1:T(8,128)(2,1)}, u32[]{:S(2)}) %copy-start) | copy-done | bytes 786456
  1.9 0.0 copy-start.1
  1.9 1.0 %copy-done.1 = f32[128,1024]{1,0:T(8,128)S(1)} copy-done((f32[128,1024]{1,0:T(8,128)S(1)}, f32[128,1024]{1,0:T(8,128)}, u32[]{:S(2)}) %copy-start.1) | copy-done | bytes 524312
  2.9 0.0 copy-start.2
  2.9 0.8 %copy-done.2 = f32[3,3,1024]{2,1,0:T(4,128)S(1)} copy-done((f32[3,3,1024]{2,1,0:T(4,128)S(1)}, f32[3,3,1024]{2,1,0:T(4,128)}, u32[]{:S(2)}) %copy-start.2) | copy-done | bytes 36888
  3.7 0.0 copy-start.3
  3.7 0.7 %copy-done.3 = bf16[1,8,1024]{2,1,0:T(8,128)(2,1)S(1)} copy-done((bf16[1,8,1024]{2,1,0:T(8,128)(2,1)S(1)}, bf16[1,8,1024]{2,1,0:T(8,128)(2,1)}, u32[]{:S(2)}) %copy-start.3) | copy-done | bytes 16408
  4.4 0.0 copy-start.4
  4.5 0.7 %copy-done.4 = f32[1024]{0:T(1024)S(1)} copy-done((f32[1024]{0:T(1024)S(1)}, f32[1024]{0:T(1024)}, u32[]{:S(2)}) %copy-start.4) | copy-done | bytes 4120
  5.1 0.0 copy-start.5
  5.1 0.7 %copy-done.5 = s32[8]{0:T(128)S(1)} copy-done((s32[8]{0:T(128)S(1)}, s32[8]{0:T(128)}, u32[]{:S(2)}) %copy-start.5) | copy-done | bytes 56
  5.8 31.3 %shard_map.100 = bf16[128,1024]{1,0:T(8,128)(2,1)S(1)} custom-call(bf16[3,128,1024]{2,1,0:T(8,128)(2,1)S(1)} %bitcast.2, bf16[1,8,1024]{2,1,0:T(8,128)(2,1)S(1)} %copy-done.3, s32[8]{0:T(128)S(1)} %copy-done.5, s32[8,4]{1,0:T(8,128)S(1)} %copy.11.pref_ref, f32[3,3,1024]{2,1,0:T(4,128)S(1)} %copy-done.2, f32[128,1024]{1,0:T(8,128)S(1)} %copy-done.1, ...), custom_call_target="tpu_custom_call" | custom-call | tf_op jit(solution)/shard_map/pallas_call | solution.py:370
  37.1 0.7 %copy.13 = bf16[128,1024]{1,0:T(8,128)(2,1)} copy(bf16[128,1024]{1,0:T(8,128)(2,1)S(1)} %shard_map.100) | data formatting | bytes 524288
Async XLA Ops:
  0.8 1.1 %copy-start = (bf16[128,3,1024]{2,0,1:T(8,128)(2,1)S(1)}, bf16[128,3,1024]{2,0,1:T(8,128)(2,1)}, u32[]{:S(2)}) copy-start(bf16[128,3,1024]{2,0,1:T(8,128)(2,1)} %param.10) | copy-start | bytes 2359300
  1.9 1.0 %copy-start.1 = (f32[128,1024]{1,0:T(8,128)S(1)}, f32[128,1024]{1,0:T(8,128)}, u32[]{:S(2)}) copy-start(f32[128,1024]{1,0:T(8,128)} %filt_ref.1) | copy-start | bytes 1572868
  2.9 0.8 %copy-start.2 = (f32[3,3,1024]{2,1,0:T(4,128)S(1)}, f32[3,3,1024]{2,1,0:T(4,128)}, u32[]{:S(2)}) copy-start(f32[3,3,1024]{2,1,0:T(4,128)} %taps_ref.1) | copy-start | bytes 110596
  3.7 0.7 %copy-start.3 = (bf16[1,8,1024]{2,1,0:T(8,128)(2,1)S(1)}, bf16[1,8,1024]{2,1,0:T(8,128)(2,1)}, u32[]{:S(2)}) copy-start(bf16[1,8,1024]{2,1,0:T(8,128)(2,1)} %lib_ref.1) | copy-start | bytes 49156
  4.4 0.7 %copy-start.4 = (f32[1024]{0:T(1024)S(1)}, f32[1024]{0:T(1024)}, u32[]{:S(2)}) copy-start(f32[1024]{0:T(1024)} %param.16) | copy-start | bytes 12292
  5.1 0.7 %copy-start.5 = (s32[8]{0:T(128)S(1)}, s32[8]{0:T(128)}, u32[]{:S(2)}) copy-start(s32[8]{0:T(128)} %slot_ref.1) | copy-start | bytes 100
where the time goes:
time: 38.1 us; the launch traced here: 37.8 us
  Pallas kernels  31.3 us (82%)
  local copies, waits for them, and re-layouts  6.49 us (17%)
    pallas_call x1, Pallas kernels, fused_body(): pl.pallas_call(functools.partial(fused_kernel, n, prefix // rows), out_sh...  31.3 us
    unnamed x14, local copies, waits for them, and re-layouts  6.49 us

commit v1 on v0

--- a/solution.py
+++ b/solution.py
@@ -132,7 +132,7 @@
 
 
 LANES = 128
-FILTER, SIGNAL, BACK, SHELF = 0, 1, 2, 3
+FILTER, SIGNAL, BACK, SHELF, ACROSS = range(5)
 
 
 def wave_tables(tokens):
@@ -146,29 +146,48 @@
 
 
 def fused_kernel(
-    n, pdev, x_ref, lib_ref, slot_ref, pref_ref, taps_ref, filt_ref, skip_ref, fhi_hbm, flo_hbm, g_hbm,
+    n, pdev, x_hbm, lib_hbm, slot_hbm, pref_hbm, taps_hbm, filt_hbm, skip_hbm, fhi_hbm, flo_hbm, g_hbm,
     out_ref,
-    fhi, flo, gmat, hsend, hrecv, ssend, srecv, ysend, yrecv, libsend, libg, lastsend, lastg,
-    halosend, halorecv, ext, gate, cach, hspec, prod,
+    x_ref, lib_ref, slot_ref, pref_ref, taps_ref, filt_ref, skip_ref, fhi, flo, gmat, hsend, hrecv, ssend, srecv, ysend, yrecv, libsend, libg, lastsend, lastg,
+    halosend, halorecv, ext, gate, cach, hspec, prod, rising,
     load_sem, send_sem, recv_sem, halo_send, halo_recv, last_send, last_recv,
 ):
     f32, bf16 = jnp.float32, jnp.bfloat16
     rows = x_ref.shape[1]
     tokens = rows * n
     prefix = pdev * rows
+    duo = rows // 2
+    steps = tokens // 2
+    phases = range(2)
+    wide = [slice(p * LANES, (p + 1) * LANES) for p in phases]
     me = lax.axis_index("seq")
-    loads = [
-        pltpu.make_async_copy(src, dst, load_sem.at[i])
-        for i, (src, dst) in enumerate([(fhi_hbm, fhi), (flo_hbm, flo), (g_hbm, gmat)])
-    ]
-    for load in loads:
-        load.start()
-
+    group = lax.axis_index("group")
+    share = rows // 4
     barrier = pltpu.get_barrier_semaphore()
     for d in range(1, n):
         pl.semaphore_signal(
             barrier, inc=1, device_id={"seq": lax.rem(me + d, n)}, device_id_type=pl.DeviceIdType.MESH
         )
+    pl.semaphore_signal(
+        barrier, inc=1, device_id={"group": 1 - group}, device_id_type=pl.DeviceIdType.MESH
+    )
+    operands = [
+        *((filt_hbm.at[:, j * LANES : (j + 1) * LANES], filt_ref.at[j]) for j in range(n)), (x_hbm, x_ref), (lib_hbm, lib_ref), (taps_hbm, taps_ref),
+        (slot_hbm, slot_ref), (pref_hbm, pref_ref), (skip_hbm, skip_ref),
+        (fhi_hbm, fhi), (flo_hbm, flo), (g_hbm, gmat),
+    ]
+    loads = [pltpu.make_async_copy(src, dst, load_sem.at[i]) for i, (src, dst) in enumerate(operands)]
+    for load in loads:
+        load.start()
+    load_filter, load_x, load_small, load_tables = loads[:n], loads[n], loads[n + 1 : -3], loads[-3:]
+
+    half_ring = n // 2
+    order = [half_ring] + [d for k in range(1, half_ring) for d in (half_ring + k, half_ring - k)]
+
+    def lanes_of(index):
+        if isinstance(index, int):
+            return pl.ds(index * LANES, LANES)
+        return pl.ds(pl.multiple_of(index * LANES, LANES), LANES)
 
     def remote(src, dst, send, recv, peer):
         return pltpu.make_async_remote_copy(
@@ -177,12 +196,25 @@
         )
 
     def at_rows(ref, index):
-        return ref.at[pl.ds(pl.multiple_of(index * rows, rows), rows)]
+        return ref.at[pl.ds(pl.multiple_of(index * duo, duo), duo)]
+
+    def at_share(ref, index):
+        return ref.at[pl.ds(pl.multiple_of(index * duo + group * share, share), share)]
+
+    def across(d):
+        part = at_share(hrecv, lax.rem(me + n - d, n))
+        return pltpu.make_async_remote_copy(
+            src_ref=part, dst_ref=part, send_sem=send_sem.at[ACROSS, d], recv_sem=recv_sem.at[ACROSS, d],
+            device_id={"group": 1 - group}, device_id_type=pl.DeviceIdType.MESH,
+        )
 
     def move(kind, d):
         peer = lax.rem(me + d, n)
         source, target = {
-            FILTER: (hsend.at[peer], at_rows(hrecv, me)),
+            FILTER: (
+                hsend.at[peer, pl.ds(pl.multiple_of(group * share, share), share)],
+                at_share(hrecv, me),
+            ),
             SIGNAL: (ssend.at[peer], at_rows(srecv, me)),
             BACK: (ysend.at[peer], yrecv.at[me]),
             SHELF: (libsend.at[peer], libg.at[me]),
@@ -199,19 +231,31 @@
         s: remote(lastsend, lastg.at[me], last_send, last_recv.at[s], pdev) for s in others
     }
 
+    def strided(start, count):
+        return pl.ds(start, count, stride=2)
+
+    for j in range(n):
+        load_filter[j].wait()
+        for p in phases:
+            hsend[j, :, wide[p]] = filt_ref[j, strided(p, duo), :].astype(bf16)
+    at_rows(hrecv, me)[...] = hsend[me]
+    load_x.wait()
     for j in range(3):
+        for c in range(n):
+            ext[j, c, 8:] = x_ref[j, :, c * LANES : (c + 1) * LANES].astype(f32)
         halosend[2 * j : 2 * j + 2] = x_ref[j, rows - 16 :].astype(f32)[14:]
     halosend[6:] = jnp.zeros((2, halosend.shape[1]), f32)
+    for load in load_small:
+        load.wait()
     shelf = lib_ref[0].astype(f32)
     for j in range(n):
         cols = slice(j * LANES, (j + 1) * LANES)
         libsend[j] = shelf[:, cols]
         lastsend[2 * j : 2 * j + 2] = shelf[6:, cols]
-        hsend[j] = filt_ref[:, cols].astype(bf16)
     libg[me] = libsend[me]
     lastg[me] = lastsend[...]
 
-    pl.semaphore_wait(barrier, n - 1)
+    pl.semaphore_wait(barrier, n)
 
     @pl.when(me < n - 1)
     def _():
@@ -222,14 +266,10 @@
         def _():
             last_copy[s].start()
 
-    for d in range(1, n):
+    for d in order:
+        move(FILTER, d).start()
+    for d in order:
         move(SHELF, d).start()
-    for d in range(1, n):
-        move(FILTER, d).start()
-    at_rows(hrecv, me)[...] = hsend[me]
-    for j in range(3):
-        ext[j, 8:] = x_ref[j].astype(f32)
-
     @pl.when(me == 0)
     def _():
         halorecv[...] = jnp.zeros_like(halorecv)
@@ -239,12 +279,13 @@
         halo_copy.wait_recv()
 
     for j in range(3):
-        ext[j, 6:8] = halorecv[2 * j : 2 * j + 2]
-
-    per_row = pref_ref.shape[1]
+        for c in range(n):
+            ext[j, c, 6:8] = halorecv[2 * j : 2 * j + 2, c * LANES : (c + 1) * LANES]
+
+    per_row = pref_ref.shape[0]
 
     def wanted(b):
-        return slot_ref[pref_ref[b // per_row, b % per_row]]
+        return slot_ref[pref_ref[b % per_row, b // per_row]]
 
     blocks = prefix // BLK
 
@@ -254,95 +295,127 @@
             last_copy[s].wait_recv()
         ends = lastg[wanted(blocks - 1)]
         for j in range(n):
-            ext[2, 6:8, j * LANES : (j + 1) * LANES] = ends[2 * j : 2 * j + 2]
-
-    def short(j, cols):
+            ext[2, j, 6:8] = ends[2 * j : 2 * j + 2]
+
+    def short(j, p, index):
+        cols = lanes_of(index)
         return (
-            taps_ref[0, j : j + 1, cols] * ext[j, 8:, cols]
-            + taps_ref[1, j : j + 1, cols] * ext[j, 7 : 7 + rows, cols]
-            + taps_ref[2, j : j + 1, cols] * ext[j, 6 : 6 + rows, cols]
+            taps_ref[0, j : j + 1, cols] * ext[j, index, strided(8 + p, duo), :]
+            + taps_ref[1, j : j + 1, cols] * ext[j, index, strided(7 + p, duo), :]
+            + taps_ref[2, j : j + 1, cols] * ext[j, index, strided(6 + p, duo), :]
         )
 
     in_prefix = me < pdev
-    for j in range(n):
-        cols = slice(j * LANES, (j + 1) * LANES)
-        factor = jnp.where(in_prefix, jnp.float32(1.0), short(2, cols))
-        ssend[j] = (short(1, cols) * factor).astype(bf16)
+
+    def pack_signal(index):
+        for p in phases:
+            factor = jnp.where(in_prefix, jnp.float32(1.0), short(2, p, index))
+            ssend[index, :, wide[p]] = (short(1, p, index) * factor).astype(bf16)
+
+    for d in order:
+        pack_signal(lax.rem(me + d, n))
+        move(SIGNAL, d).start()
+    pack_signal(me)
+    at_rows(srecv, me)[...] = ssend[me]
     for d in range(1, n):
-        move(SIGNAL, d).start()
-    at_rows(srecv, me)[...] = ssend[me]
-    for j in range(n):
-        cols = slice(j * LANES, (j + 1) * LANES)
-        gate[:, cols] = short(0, cols)
-
-    own = pl.ds(pl.multiple_of(me * LANES, LANES), LANES)
+        move(FILTER, d).wait_recv()
+        across(d).start()
+
+    own = lanes_of(me)
     arrived(SHELF)
     cach[:8] = jnp.zeros((8, LANES), f32)
     for b in range(blocks):
         cach[8 + BLK * b : 8 + BLK * (b + 1)] = libg[wanted(b)]
 
-    arrived(FILTER)
-    for load in loads:
+    for d in range(1, n):
+        across(d).wait_recv()
+    for load in load_tables:
         load.wait()
-    tile = 512
-    skip = skip_ref[:, own]
+    tile = 256
+    skip = skip_ref[own].reshape(1, LANES)
 
     def filter_tile(i, carry):
         span = pl.ds(pl.multiple_of(i * tile, tile), tile)
         spec = jnp.dot(fhi[span], hrecv[...], preferred_element_type=f32)
         spec += jnp.dot(flo[span], hrecv[...], preferred_element_type=f32)
-        hspec[span] = spec + jnp.where(i < tokens // tile, skip, 0.0)
+        hspec[span, wide[0]] = spec[:, wide[0]] + jnp.where(i < steps // tile, skip, 0.0)
+        hspec[span, wide[1]] = spec[:, wide[1]]
         return carry
 
-    lax.fori_loop(0, 2 * tokens // tile, filter_tile, 0)
-
+    lax.fori_loop(0, 2 * steps // tile, filter_tile, 0)
+
+    for j in range(n):
+        for p in phases:
+            gate[j, :, wide[p]] = short(0, p, j)
+
+    early = prefix // 2
+    cached = [
+        taps_ref[0, 2:3, own] * cach[strided(8 + p, early), :]
+        + taps_ref[1, 2:3, own] * cach[strided(7 + p, early), :]
+        + taps_ref[2, 2:3, own] * cach[strided(6 + p, early), :]
+        for p in phases
+    ]
     arrived(SIGNAL)
-    cached = (
-        taps_ref[0, 2:3, own] * cach[8:]
-        + taps_ref[1, 2:3, own] * cach[7 : 7 + prefix]
-        + taps_ref[2, 2:3, own] * cach[6 : 6 + prefix]
-    )
-    srecv[:prefix] = (srecv[:prefix].astype(f32) * cached).astype(bf16)
-
-    half = 256
+    for p in phases:
+        srecv[:early, wide[p]] = (srecv[:early, wide[p]].astype(f32) * cached[p]).astype(bf16)
+
+    half = 128
+
+    def times(first, second):
+        return (
+            first[0] * second[0] - first[1] * second[1],
+            first[0] * second[1] + first[1] * second[0],
+        )
 
     def signal_tile(i, carry):
-        upper = pl.ds(pl.multiple_of(i * half, half), half)
-        lower = pl.ds(pl.multiple_of(tokens + i * half, half), half)
-        even = jnp.dot(fhi[upper], srecv[...], preferred_element_type=f32)
-        even += jnp.dot(flo[upper], srecv[...], preferred_element_type=f32)
-        odd = jnp.dot(fhi[lower], srecv[...], preferred_element_type=f32)
-        odd += jnp.dot(flo[lower], srecv[...], preferred_element_type=f32)
-        tap_even, tap_odd = hspec[upper] * (1.0 / tokens), hspec[lower] * (1.0 / tokens)
-        for span, value in (
-            (upper, even * tap_even - odd * tap_odd),
-            (lower, even * tap_odd + odd * tap_even),
-        ):
-            high = value.astype(bf16)
-            prod[span, :LANES] = high
-            prod[span, LANES:] = (value - high.astype(f32)).astype(bf16)
+        spans = [pl.ds(pl.multiple_of(part * steps + i * half, half), half) for part in range(2)]
+        waves = [
+            jnp.dot(fhi[span], srecv[...], preferred_element_type=f32)
+            + jnp.dot(flo[span], srecv[...], preferred_element_type=f32)
+            for span in spans
+        ]
+        taps = [hspec[span] * (1.0 / steps) for span in spans]
+        turn = [fhi[span, 1:2].astype(f32) + flo[span, 1:2].astype(f32) for span in spans]
+        even, odd = ([wave[:, wide[p]] for wave in waves] for p in phases)
+        tap_even, tap_odd = ([tap[:, wide[p]] for tap in taps] for p in phases)
+        late = times(times(odd, tap_odd), turn)
+        even_even, even_odd, odd_even = times(even, tap_even), times(even, tap_odd), times(odd, tap_even)
+        for part in range(2):
+            for p, value in ((0, even_even[part] + late[part]), (1, even_odd[part] + odd_even[part])):
+                high = value.astype(bf16)
+                prod[spans[part], wide[p]] = high
+                prod[spans[part], (2 + p) * LANES : (3 + p) * LANES] = (
+                    value - high.astype(f32)
+                ).astype(bf16)
         return carry
 
-    lax.fori_loop(0, tokens // half, signal_tile, 0)
-
-    pair = 2 * rows
-
-    def back_tile(i, carry):
-        span = pl.ds(pl.multiple_of(i * pair, pair), pair)
+    lax.fori_loop(0, steps // half, signal_tile, 0)
+
+    reach = half_ring * duo
+    for k in (1, 0):
+        side = lax.rem(me // half_ring + k, 2)
+        span = pl.ds(pl.multiple_of(side * reach, reach), reach)
         both = jnp.dot(gmat[span], prod[...], preferred_element_type=f32)
-        value = (both[:, :LANES] + both[:, LANES:]).astype(bf16)
-        ysend[2 * i] = value[:rows]
-        ysend[2 * i + 1] = value[rows:]
-        return carry
-
-    lax.fori_loop(0, n // 2, back_tile, 0)
+        value = (both[:, : 2 * LANES] + both[:, 2 * LANES :]).astype(bf16)
+        for r in range(half_ring):
+            target = side * half_ring + r
+            ysend[target] = value[r * duo : (r + 1) * duo]
+
+            @pl.when(target != me)
+            def _():
+                move(BACK, lax.rem(target - me + n, n)).start()
+
+    def finish(source, value):
+        cols = lanes_of(source)
+        for p in phases:
+            rising[strided(p, duo), :] = gate[source, :, wide[p]] * value[:, wide[p]].astype(f32)
+        out_ref[:, cols] = rising[...].astype(bf16)
+
+    finish(me, ysend[me])
     for d in range(1, n):
-        move(BACK, d).start()
-    yrecv[me] = ysend[me]
-    arrived(BACK)
-    for j in range(n):
-        cols = slice(j * LANES, (j + 1) * LANES)
-        out_ref[:, cols] = (gate[:, cols] * yrecv[j].astype(f32)).astype(bf16)
+        move(BACK, d).wait_recv()
+        source = lax.rem(me + n - d, n)
+        finish(source, yrecv[source])
 
     @pl.when(me < n - 1)
     def _():
@@ -355,6 +428,8 @@
     for kind in (SHELF, FILTER, SIGNAL, BACK):
         for d in range(1, n):
             move(kind, d).wait_send()
+    for d in range(1, n):
+        across(d).wait_send()
 
 
 def fused_body(n, fresh, library, block_slot, prefix_blocks, short_taps, long_filter, skip_gain):
@@ -362,64 +437,72 @@
     tokens = rows * n
     prefix = prefix_blocks.size * BLK
     f32, bf16 = jnp.float32, jnp.bfloat16
-    high, low, turned = wave_tables(tokens)
-    vmem = pl.BlockSpec(memory_space=pltpu.VMEM)
-    smem = pl.BlockSpec(memory_space=pltpu.SMEM)
-    far = pl.BlockSpec(memory_space=pl.ANY)
+    high, low, turned = wave_tables(tokens // 2)
+    far = pl.BlockSpec(memory_space=pltpu.HBM)
     dma = pltpu.SemaphoreType.DMA
     return pl.pallas_call(
         functools.partial(fused_kernel, n, prefix // rows),
         out_shape=jax.ShapeDtypeStruct((rows, channels), bf16),
-        in_specs=[vmem, vmem, smem, smem, vmem, vmem, vmem, far, far, far],
-        out_specs=vmem,
+        in_specs=[far] * 10,
+        out_specs=pl.BlockSpec(memory_space=pltpu.VMEM),
         scratch_shapes=[
-            pltpu.VMEM((2 * tokens, tokens), bf16),
-            pltpu.VMEM((2 * tokens, tokens), bf16),
-            pltpu.VMEM((tokens, 2 * tokens), bf16),
-            pltpu.VMEM((n, rows, LANES), bf16),
-            pltpu.VMEM((tokens, LANES), bf16),
-            pltpu.VMEM((n, rows, LANES), bf16),
-            pltpu.VMEM((tokens, LANES), bf16),
-            pltpu.VMEM((n, rows, LANES), bf16),
-            pltpu.VMEM((n, rows, LANES), bf16),
+            pltpu.VMEM((3, rows, channels), bf16),
+            pltpu.VMEM(library.shape, bf16),
+            pltpu.SMEM(block_slot.shape, jnp.int32),
+            pltpu.SMEM(prefix_blocks.shape[::-1], jnp.int32),
+            pltpu.VMEM(short_taps.shape, f32),
+            pltpu.VMEM((n, rows, LANES), f32),
+            pltpu.VMEM(skip_gain.shape, f32),
+            pltpu.VMEM((tokens, tokens // 2), bf16),
+            pltpu.VMEM((tokens, tokens // 2), bf16),
+            pltpu.VMEM((tokens // 2, tokens), bf16),
+            pltpu.VMEM((n, rows // 2, 2 * LANES), bf16),
+            pltpu.VMEM((tokens // 2, 2 * LANES), bf16),
+            pltpu.VMEM((n, rows // 2, 2 * LANES), bf16),
+            pltpu.VMEM((tokens // 2, 2 * LANES), bf16),
+            pltpu.VMEM((n, rows // 2, 2 * LANES), bf16),
+            pltpu.VMEM((n, rows // 2, 2 * LANES), bf16),
             pltpu.VMEM((n, BLK, LANES), f32),
             pltpu.VMEM((n, BLK, LANES), f32),
             pltpu.VMEM((2 * n, LANES), f32),
             pltpu.VMEM((n, 2 * n, LANES), f32),
             pltpu.VMEM((8, channels), f32),
             pltpu.VMEM((8, channels), f32),
-            pltpu.VMEM((3, rows + 8, channels), f32),
-            pltpu.VMEM((rows, channels), f32),
+            pltpu.VMEM((3, n, rows + 8, LANES), f32),
+            pltpu.VMEM((n, rows // 2, 2 * LANES), f32),
             pltpu.VMEM((prefix + 8, LANES), f32),
-            pltpu.VMEM((2 * tokens, LANES), f32),
-            pltpu.VMEM((2 * tokens, 2 * LANES), bf16),
-            dma((3,)),
-            dma((4, n)),
-            dma((4, n)),
+            pltpu.VMEM((tokens, 2 * LANES), f32),
+            pltpu.VMEM((tokens, 4 * LANES), bf16),
+            pltpu.VMEM((rows, LANES), f32),
+            dma((9 + n,)),
+            dma((5, n)),
+            dma((5, n)),
             dma(()),
             dma(()),
             dma(()),
             dma((n,)),
         ],
         compiler_params=pltpu.CompilerParams(
-            collective_id=0, has_side_effects=True, vmem_limit_bytes=50 * 1024 * 1024
+            collective_id=0, has_side_effects=True, vmem_limit_bytes=63 * 1024 * 1024
         ),
     )(
-        jnp.transpose(fresh, (1, 0, 2)), library, block_slot, prefix_blocks, short_taps, long_filter,
-        skip_gain[None, :], jnp.asarray(high), jnp.asarray(low), jnp.asarray(turned),
-    )
-
-
-def body(n, fresh, library, block_slot, prefix_blocks, short_taps, long_filter, skip_gain):
+        jnp.transpose(fresh, (1, 0, 2)), library, block_slot, prefix_blocks.T, short_taps, long_filter,
+        skip_gain, jnp.asarray(high), jnp.asarray(low), jnp.asarray(turned),
+    )
+
+
+def body(groups, n, fresh, library, block_slot, prefix_blocks, short_taps, long_filter, skip_gain):
     rows, channels = fresh.shape[0], fresh.shape[2]
     prefix = prefix_blocks.size * BLK
     small = (
-        rows * n <= 1024
+        groups == 2
+        and rows * n <= 1024
         and rows % 128 == 0
         and channels == n * LANES
         and library.shape[0] == 1
         and prefix % rows == 0
-        and 0 < prefix // rows < n
+        and 0 < prefix // rows <= n // 2
+        and n % 2 == 0
     )
     chosen = functools.partial(fused_body, n) if small else long_body
     return chosen(fresh, library, block_slot, prefix_blocks, short_taps, long_filter, skip_gain)
@@ -427,7 +510,7 @@
 
 def solution(mesh):
     return jax.shard_map(
-        functools.partial(body, mesh.shape["seq"]),
+        functools.partial(body, mesh.shape["group"], mesh.shape["seq"]),
         mesh=mesh,
         in_specs=(
             P(("group", "seq"), None, "chan"),

time: 38.1 us -> 28 us (0.73)
  Pallas kernels: 31.3 us -> 26.2 us
  local copies, waits for them, and re-layouts: 6.49 us -> 1.67 us
    pallas_call x1, Pallas kernels: 31.3 us -> 26.2 us  [fused_body(): pl.pallas_call(functools.partial(fused_kernel, n, prefix // rows), out_sh...]
    unnamed x14 -> x1, local copies, waits for them, and re-layouts: 6.49 us -> 1.67 us
where the time goes in v1:
time: 28 us; the launch traced here: 27.8 us
  Pallas kernels  26.2 us (94%)
  local copies, waits for them, and re-layouts  1.67 us (6%)
    pallas_call x1, Pallas kernels, fused_body(): pl.pallas_call(functools.partial(fused_kernel, n, prefix // rows), out_sh...  26.2 us
    unnamed x1, local copies, waits for them, and re-layouts  1.67 us

profile of v1, /device:TPU:0, one launch (start us, length us, event | category | flops | bytes accessed | tf_op | source)
XLA Modules:
  0.0 27.8 jit_solution(10129749401569986489)
XLA Ops:
  0.0 26.2 %shard_map.100 = bf16[128,1024]{1,0:T(8,128)(2,1)} custom-call(bf16[3,128,1024]{2,1,0:T(8,128)(2,1)} %bitcast.2, bf16[1,8,1024]{2,1,0:T(8,128)(2,1)} %lib_hbm.1, s32[8]{0:T(128)} %slot_hbm.1, s32[4,8]{1,0:T(4,128)} %bitcast.3, f32[3,3,1024]{2,1,0:T(4,128)} %taps_hbm.1, f32[128,1024]{1,0:T(8,128)} %filt_hbm.1, f32[1024]{0:T(1024)} %skip_hbm.1, ...), custom_call_target="tpu_custom_call" | custom-call | tf_op jit(solution)/shard_map/pallas_call | solution.py:443
  26.2 1.7 %copy.12 = bf16[128,1024]{1,0:T(8,128)(2,1)} copy(bf16[128,1024]{1,0:T(8,128)(2,1)} %shard_map.100) | data formatting | bytes 524288

commit v2 on v1

--- a/solution.py
+++ b/solution.py
@@ -182,7 +182,7 @@
     load_filter, load_x, load_small, load_tables = loads[:n], loads[n], loads[n + 1 : -3], loads[-3:]
 
     half_ring = n // 2
-    order = [half_ring] + [d for k in range(1, half_ring) for d in (half_ring + k, half_ring - k)]
+    order = [d for k in range(1, half_ring) for d in (k, n - k)] + [half_ring]
 
     def lanes_of(index):
         if isinstance(index, int):

time: 28 us -> 27.4 us (0.979)
  Pallas kernels: 26.2 us -> 25.6 us
    pallas_call x1, Pallas kernels: 26.2 us -> 25.6 us  [fused_body(): pl.pallas_call(functools.partial(fused_kernel, n, prefix // rows), out_sh...]
where the time goes in v2:
time: 27.4 us; the launch traced here: 27.3 us
  Pallas kernels  25.6 us (93%)
  local copies, waits for them, and re-layouts  1.67 us (6%)
    pallas_call x1, Pallas kernels, fused_body(): pl.pallas_call(functools.partial(fused_kernel, n, prefix // rows), out_sh...  25.6 us
    unnamed x1, local copies, waits for them, and re-layouts  1.67 us

profile of v2, /device:TPU:0, one launch (start us, length us, event | category | flops | bytes accessed | tf_op | source)
XLA Modules:
  0.0 27.3 jit_solution(13535576916549425358)
XLA Ops:
  0.0 25.6 %shard_map.100 = bf16[128,1024]{1,0:T(8,128)(2,1)} custom-call(bf16[3,128,1024]{2,1,0:T(8,128)(2,1)} %bitcast.2, bf16[1,8,1024]{2,1,0:T(8,128)(2,1)} %lib_hbm.1, s32[8]{0:T(128)} %slot_hbm.1, s32[4,8]{1,0:T(4,128)} %bitcast.3, f32[3,3,1024]{2,1,0:T(4,128)} %taps_hbm.1, f32[128,1024]{1,0:T(8,128)} %filt_hbm.1, f32[1024]{0:T(1024)} %skip_hbm.1, ...), custom_call_target="tpu_custom_call" | custom-call | tf_op jit(solution)/shard_map/pallas_call | solution.py:443
  25.6 1.7 %copy.12 = bf16[128,1024]{1,0:T(8,128)(2,1)} copy(bf16[128,1024]{1,0:T(8,128)(2,1)} %shard_map.100) | data formatting | bytes 524288
